TPU v7x, 256 devices: a whole 4x4x8 slice. The times are simulated.
256 devices in a mesh: lat: 16 (over x_lo, y, core), lon: 16 (over x_hi, z).
Axes of the slice: x: 4 (x_hi: 2, x_lo: 2; x = x_hi * 2 + x_lo), y: 4, z: 8, core: 2. Of those that a mesh axis runs over, the one named last changes fastest.
Arguments:
- obs_frac: float32 [16, 16, 2, 1024], P('lat', 'lon'), may hold values from 0 to 1
- obs_field: float32 [16, 16, 3, 1024], P('lat', 'lon'), may hold values from -6 to 6
- dipole_frac: float32 [16, 16, 2, 256], P('lat', 'lon'), may hold values from 0 to 1
- dipole_moment: float32 [16, 16, 256], P('lat', 'lon'), may hold values from -6 to 6
- obs_count: int32 [16, 16], P('lat', 'lon'), may hold values from 256 to 1024, as said below
Outputs:
- gram: float32 [16, 16, 13, 256, 256], P('lat', 'lon')
- rhs: float32 [16, 16, 256], P('lat', 'lon')
Inputs may be any that keep to these rules, and one draw needn't show every extreme that they name: `obs_count`: tiles of the first and of the last latitude row hold exactly 1024 observations; every other tile holds between 256 and 512.
All inputs are finite; a program needn't handle non-finite values.
Results may differ from a plain program's by a relative error of at most 0.0003.
Values sent between devices are 32-bit elements; how exact they have to be, the bound alone decides.
A program may use at most 128 MiB of HBM per device.

v0:
```python
import functools
import math

import jax
import jax.numpy as jnp
import numpy as np
from jax import lax
from jax.experimental import pallas as pl
from jax.experimental.pallas import tpu as pltpu
from jax.sharding import PartitionSpec as P

CROSS = ((0, 0), (-1, 0), (1, 0), (0, -1), (0, 1))
OFFSETS = (
    (0, 0),
    (-1, 0),
    (1, 0),
    (0, -1),
    (0, 1),
    (-2, 0),
    (2, 0),
    (0, -2),
    (0, 2),
    (-1, -1),
    (-1, 1),
    (1, -1),
    (1, 1),
)
OBS_RADIUS = 1.06
SOURCE_RADIUS = 0.99
KERNEL_SCALE = 0.0001
HUBER_EDGE = 0.8
DEGREE = math.pi / 180.0
LAT = 16
LON = 16
BS = 256
OBS = 1024
HALF = 512
SPARE = 13
EDGE = (1.5 * (OBS_RADIUS**2 + SOURCE_RADIUS**2) - 3.0 * SOURCE_RADIUS**2) / 1.5
FOLD = 1.5 * KERNEL_SCALE * EDGE**-1.5
FEATURES = 32
FIELDS = 8


def pass_table():
    table = np.zeros((LAT, 8, FIELDS), np.int32)
    counts = np.zeros((LAT,), np.int32)
    for lat in range(LAT):
        rows = []
        for slot, (lat_step, lon_step) in enumerate(CROSS):
            tile = lat - lat_step
            if not 0 <= tile < LAT:
                continue
            there = [b for b in CROSS if 0 <= tile + b[0] < LAT]
            there.sort(key=lambda b: b != (lat_step, lon_step))
            blocks = [OFFSETS.index((b[0] - lat_step, b[1] - lon_step)) for b in there]
            blocks += [SPARE] * (5 - len(blocks))
            for half in range(2 if tile in (0, LAT - 1) else 1):
                rows.append([slot, half] + blocks + [len(there)])
        counts[lat] = len(rows)
        table[lat, : len(rows)] = rows
    return table, counts


def positions(angles, radius):
    cosine, sine = jnp.cos(angles), jnp.sin(angles)
    ring = radius * cosine[0:1]
    return ring * cosine[1:2], ring * sine[1:2], radius * sine[0:1]


def exchange(count_ref, obs_ref, field_ref, dip_ref, moment_ref, dips, tiles, origin, send_dip, recv_dip, send_obs, recv_obs):
    lat, lon = lax.axis_index("lat"), lax.axis_index("lon")

    def inside(step):
        return (lat + step >= 0) & (lat + step < LAT)

    def device(offset):
        return (lat + offset[0], lax.rem(lon + offset[1] + LON, LON))

    barrier = pltpu.get_barrier_semaphore()
    for offset in OFFSETS[1:]:

        @pl.when(inside(offset[0]))
        def _():
            pl.semaphore_signal(barrier, inc=1, device_id=device(offset), device_id_type=pl.DeviceIdType.MESH)

    def angles(fraction):
        row = lax.broadcasted_iota(jnp.int32, fraction.shape, 0)
        index = jnp.where(row == 0, lat.astype(jnp.float32), lon.astype(jnp.float32))
        span = jnp.where(row == 0, 160.0 * DEGREE / LAT, 2.0 * math.pi / LON)
        base = jnp.where(row == 0, -80.0 * DEGREE, 0.0)
        return base + (index + fraction) * span

    for row, value in enumerate(positions(angles(dip_ref[...]), SOURCE_RADIUS)):
        dips[0, row : row + 1, :] = value
    dips[0, 3:4, :] = moment_ref[...]
    dips[0, 4:8, :] = jnp.zeros((4, BS), jnp.float32)
    dips[SPARE] = jnp.zeros((8, BS), jnp.float32)
    for row, value in enumerate(positions(angles(obs_ref[...]), OBS_RADIUS)):
        tiles[0, row : row + 1, :] = value
    tiles[0, 3:6, :] = field_ref[...]
    slot_index = lax.broadcasted_iota(jnp.int32, (1, OBS), 1)
    tiles[0, 6:7, :] = jnp.where(slot_index < count_ref[0, 0], 1.0, 0.0)
    tiles[0, 7:8, :] = jnp.zeros((1, OBS), jnp.float32)
    origin[...] = jnp.zeros_like(origin)
    for row, value in enumerate(positions(angles(jnp.full((2, 128), 0.5, jnp.float32)), 0.5 * (OBS_RADIUS + SOURCE_RADIUS))):
        origin[row : row + 1, :] = value

    pl.semaphore_wait(barrier, sum(inside(offset[0]).astype(jnp.int32) for offset in OFFSETS[1:]))

    def dip_copy(slot):
        step = OFFSETS[slot]
        return pltpu.make_async_remote_copy(
            src_ref=dips.at[0],
            dst_ref=dips.at[slot],
            send_sem=send_dip.at[slot],
            recv_sem=recv_dip.at[slot],
            device_id=device((-step[0], -step[1])),
            device_id_type=pl.DeviceIdType.MESH,
        )

    def obs_copy(slot):
        return pltpu.make_async_remote_copy(
            src_ref=tiles.at[0],
            dst_ref=tiles.at[slot],
            send_sem=send_obs.at[slot],
            recv_sem=recv_obs.at[slot],
            device_id=device(CROSS[slot]),
            device_id_type=pl.DeviceIdType.MESH,
        )

    for slot in range(1, len(CROSS)):

        @pl.when(inside(CROSS[slot][0]))
        def _():
            obs_copy(slot).start()

    for slot in range(1, len(OFFSETS)):

        @pl.when(inside(-OFFSETS[slot][0]))
        def _():
            dip_copy(slot).start()

    for slot in range(1, len(OFFSETS)):

        @pl.when(inside(OFFSETS[slot][0]))
        def _():
            dip_copy(slot).wait_recv()

        @pl.when(jnp.logical_not(inside(OFFSETS[slot][0])))
        def _():
            dips[slot] = jnp.zeros((8, BS), jnp.float32)

        @pl.when(inside(-OFFSETS[slot][0]))
        def _():
            dip_copy(slot).wait_send()

    for slot in range(1, len(CROSS)):

        @pl.when(inside(-CROSS[slot][0]))
        def _():
            obs_copy(slot).wait_recv()

        @pl.when(jnp.logical_not(inside(-CROSS[slot][0])))
        def _():
            tiles[slot] = jnp.zeros((8, OBS), jnp.float32)

        @pl.when(inside(CROSS[slot][0]))
        def _():
            obs_copy(slot).wait_send()


def thirds(value):
    high = value.astype(jnp.bfloat16).astype(jnp.float32)
    rest = value - high
    middle = rest.astype(jnp.bfloat16).astype(jnp.float32)
    return high, middle, rest - middle


def fill(slabs, parts, squares, flipped):
    high, middle, low = parts
    order = (high, middle, high, low, middle, high) if flipped else (high, high, middle, high, middle, low)
    for row, part in enumerate(order):
        slabs[3 * row : 3 * row + 3, :] = part
    ones = jnp.ones_like(squares[0])
    tail = (ones, ones, ones) + squares if flipped else squares + (ones, ones, ones)
    for row, part in enumerate(tail):
        slabs[18 + row : 19 + row, :] = part
    slabs[24:32, :] = jnp.zeros((8, slabs.shape[1]), jnp.float32)


def couple(squared, points, sources):
    inverse = lax.rsqrt(squared)
    second = inverse * inverse
    third = inverse * second
    fifth = third * second
    along = fifth - third
    across = fifth - third * (1.0 / 3.0)
    return [along * p - across * s for p, s in zip(points, sources)]


def compute(counts, table, dips, tiles, origin, gram, rhs, obs_rows, obs_features, source_features, wide, squared, low, own, weighted, predicted, right, total, slab_s, slab_o, out_sem):
    lat = lax.axis_index("lat")
    passes = counts[lat]
    centre = origin[0:3, 0:1]

    def source_setup(slot, carry):
        raw = dips[slot]
        local = raw[0:3, :] - centre
        scaled = local * (-2.0 / EDGE)
        square = jnp.sum(local * local, axis=0, keepdims=True) * (1.0 / EDGE)
        fill(slab_s, thirds(scaled), thirds(square), True)
        source_features[slot] = slab_s[...].T.astype(jnp.bfloat16)
        columns = raw.T
        for row in range(4):
            column = columns[:, row : row + 1] * (FOLD if row < 3 else 1.0)
            wide[slot, row] = jnp.broadcast_to(column, (BS, 128))
        return carry

    lax.fori_loop(0, 14, source_setup, 0)

    def obs_setup(slot, carry):
        raw = tiles[slot]
        local = raw[0:3, :] - centre
        square = jnp.sum(local * local, axis=0, keepdims=True) * (1.0 / EDGE)
        fill(slab_o, thirds(local), thirds(square), False)
        features = slab_o[...].astype(jnp.bfloat16)
        obs_features[slot, 0] = features[:, :HALF]
        obs_features[slot, 1] = features[:, HALF:]
        scaled = raw[0:3, :] * FOLD
        for half in range(2):
            obs_rows[slot, half, 0:3, :] = scaled[:, half * HALF : (half + 1) * HALF]
            obs_rows[slot, half, 3:7, :] = raw[3:7, half * HALF : (half + 1) * HALF]
        return carry

    lax.fori_loop(0, 5, obs_setup, 0)

    total[...] = jnp.zeros_like(total)
    right[...] = jnp.zeros_like(right)

    def square_block(tile, half, source, to):
        squared[to] = jnp.dot(source_features[source], obs_features[tile, half], preferred_element_type=jnp.float32)

    def couple_block(tile, half, source, position):
        for lane in range(4):
            lanes = slice(lane * 128, lane * 128 + 128)
            points = [obs_rows[tile, half, c : c + 1, lanes] for c in range(3)]
            sums = [jnp.zeros((16, 128), jnp.float32) for c in range(3)]
            for piece in range(16):
                rows = slice(piece * 16, piece * 16 + 16)
                values = couple(squared[position % 3, rows, lanes], points, [wide[source, c, rows] for c in range(3)])
                moment = wide[source, 3, rows]
                for c in range(3):
                    sums[c] = sums[c] + values[c] * moment
                    columns = slice(c * HALF + lane * 128, c * HALF + lane * 128 + 128)
                    low[position, rows, columns] = values[c].astype(jnp.bfloat16)
                    if position == 0:
                        own[rows, columns] = values[c]
            for c in range(3):
                columns = slice(c * HALF + lane * 128, c * HALF + lane * 128 + 128)
                if position == 0:
                    predicted[:, columns] = sums[c]
                else:
                    predicted[:, columns] += sums[c]

    def add_gram(target, position):
        product = lax.dot_general(weighted[...], low[position], (((1,), (1,)), ((), ())), preferred_element_type=jnp.float32)
        total[target] = total[target] + product

    def one_pass(number, before):
        entry = [table[lat, number, field] for field in range(FIELDS)]
        tile, half, sources, blocks = entry[0], entry[1], entry[2:7], entry[7]
        square_block(tile, half, sources[0], 0)
        for position in range(4):
            square_block(tile, half, sources[position + 1], (position + 1) % 3)
            add_gram(before[position], position + 1)
            couple_block(tile, half, sources[position], position)

        @pl.when(blocks == 5)
        def _():
            couple_block(tile, half, sources[4], 4)

        for lane in range(4):
            lanes = slice(lane * 128, lane * 128 + 128)
            present = obs_rows[tile, half, 6:7, lanes] * HUBER_EDGE
            residual, weight = [], []
            for c in range(3):
                columns = slice(c * HALF + lane * 128, c * HALF + lane * 128 + 128)
                value = obs_rows[tile, half, 3 + c : 4 + c, lanes] - jnp.sum(predicted[:, columns], axis=0, keepdims=True)
                residual.append(value)
                weight.append(present / jnp.maximum(jnp.abs(value), HUBER_EDGE))
            for piece in range(16):
                rows = slice(piece * 16, piece * 16 + 16)
                sums = right[rows]
                for c in range(3):
                    columns = slice(c * HALF + lane * 128, c * HALF + lane * 128 + 128)
                    value = own[rows, columns] * weight[c]
                    weighted[rows, columns] = value.astype(jnp.bfloat16)
                    sums = sums + value * residual[c]
                right[rows] = sums
        add_gram(0, 0)
        return tuple(sources[1:])

    last = lax.fori_loop(0, passes, one_pass, (SPARE,) * 4)
    for position in range(4):
        add_gram(last[position], position + 1)
    rhs[...] = jnp.sum(right[...].T, axis=0, keepdims=True)
    copy = pltpu.make_async_copy(total.at[pl.ds(0, 13)], gram, out_sem)
    copy.start()
    copy.wait()


def shards(obs_frac, obs_field, dipole_frac, dipole_moment, obs_count):
    vmem = pl.BlockSpec(memory_space=pltpu.VMEM)
    smem = pl.BlockSpec(memory_space=pltpu.SMEM)
    slots = len(OFFSETS) + 1
    dips, tiles, origin = pl.pallas_call(
        exchange,
        out_shape=(
            jax.ShapeDtypeStruct((slots, 8, BS), jnp.float32),
            jax.ShapeDtypeStruct((5, 8, OBS), jnp.float32),
            jax.ShapeDtypeStruct((8, 128), jnp.float32),
        ),
        in_specs=[smem, vmem, vmem, vmem, vmem],
        out_specs=(vmem, vmem, vmem),
        scratch_shapes=[
            pltpu.SemaphoreType.DMA((len(OFFSETS),)),
            pltpu.SemaphoreType.DMA((len(OFFSETS),)),
            pltpu.SemaphoreType.DMA((len(CROSS),)),
            pltpu.SemaphoreType.DMA((len(CROSS),)),
        ],
        compiler_params=pltpu.CompilerParams(collective_id=0, has_side_effects=True),
        name="exchange",
    )(obs_count, obs_frac[0, 0], obs_field[0, 0], dipole_frac[0, 0], dipole_moment[0])
    gram, rhs = compute_call(dips, tiles, origin)
    return gram[None, None], rhs[None]


def compute_call(dips, tiles, origin, kernel=compute):
    vmem = pl.BlockSpec(memory_space=pltpu.VMEM)
    smem = pl.BlockSpec(memory_space=pltpu.SMEM)
    slots = len(OFFSETS) + 1
    table, counts = pass_table()
    f32, low = jnp.float32, jnp.bfloat16
    return pl.pallas_call(
        kernel,
        out_shape=(jax.ShapeDtypeStruct((13, BS, BS), f32), jax.ShapeDtypeStruct((1, BS), f32)),
        in_specs=[smem, smem, vmem, vmem, vmem],
        out_specs=(pl.BlockSpec(memory_space=pl.ANY), vmem),
        scratch_shapes=[
            pltpu.VMEM((5, 2, 8, HALF), f32),
            pltpu.VMEM((5, 2, FEATURES, HALF), low),
            pltpu.VMEM((slots, BS, FEATURES), low),
            pltpu.VMEM((slots, 4, BS, 128), f32),
            pltpu.VMEM((3, BS, HALF), f32),
            pltpu.VMEM((5, BS, 3 * HALF), low),
            pltpu.VMEM((BS, 3 * HALF), f32),
            pltpu.VMEM((BS, 3 * HALF), low),
            pltpu.VMEM((16, 3 * HALF), f32),
            pltpu.VMEM((BS, 128), f32),
            pltpu.VMEM((slots, BS, BS), f32),
            pltpu.VMEM((FEATURES, BS), f32),
            pltpu.VMEM((FEATURES, OBS), f32),
            pltpu.SemaphoreType.DMA,
        ],
        compiler_params=pltpu.CompilerParams(vmem_limit_bytes=48 * 2**20),
        name="normal_blocks",
    )(jnp.asarray(counts), jnp.asarray(table), dips, tiles, origin)


def solution(mesh):
    in_specs = (
        P("lat", "lon", None, None),
        P("lat", "lon", None, None),
        P("lat", "lon", None, None),
        P("lat", "lon", None),
        P("lat", "lon"),
    )
    out_specs = (P("lat", "lon", None, None, None), P("lat", "lon", None))
    return jax.shard_map(shards, mesh=mesh, in_specs=in_specs, out_specs=out_specs, check_vma=False)
```

profile of v0, /device:TPU:1, one launch (start us, length us, event | category | flops | bytes accessed | tf_op | source)
XLA Modules:
  0.0 54.4 jit_solution(1885660863743718862)
XLA Ops:
  1.3 1.3 %copy.11 = f32[1,1,3,1024]{3,2,1,0:T(4,128)} copy(f32[1,1,3,1024]{3,1,2,0:T(1,128)} %param.8) | data formatting | bytes 24576
  2.6 16.4 %exchange.1 = (f32[14,8,256]{2,1,0:T(8,128)}, f32[5,8,1024]{2,1,0:T(8,128)}, f32[8,128]{1,0:T(8,128)}) custom-call(s32[1,1]{1,0:T(1,128)S(6)} %copy.12.count_ref, f32[2,1024]{1,0:T(2,128)} %bitcast.9, f32[3,1024]{1,0:T(4,128)} %bitcast.8, f32[2,256]{1,0:T(2,128)} %bitcast.10, f32[1,256]{1,0:T(1,128)} %bitcast.11), custom_call_target="tpu_custom_call" | custom-call | tf_op jit(solution)/shard_map/exchange/pallas_call | solution.py:317
  19.0 0.0 copy-start
  19.0 0.9 %copy-done = f32[5,8,1024]{2,1,0:T(8,128)S(1)} copy-done((f32[5,8,1024]{2,1,0:T(8,128)S(1)}, f32[5,8,1024]{2,1,0:T(8,128)}, u32[]{:S(2)}) %copy-start) | copy-done | bytes 163864
  19.9 0.0 copy-start.1
  19.9 0.9 %copy-done.1 = f32[14,8,256]{2,1,0:T(8,128)S(1)} copy-done((f32[14,8,256]{2,1,0:T(8,128)S(1)}, f32[14,8,256]{2,1,0:T(8,128)}, u32[]{:S(2)}) %copy-start.1) | copy-done | bytes 114712
  20.8 0.0 copy-start.2
  20.8 0.8 %copy-done.2 = s32[16,8,8]{2,1,0:T(8,128)S(1)} copy-done((s32[16,8,8]{2,1,0:T(8,128)S(1)}, s32[16,8,8]{2,1,0:T(8,128)}, u32[]{:S(2)}) %copy-start.2) | copy-done | bytes 4120
  21.7 0.0 copy-start.3
  21.7 0.7 %copy-done.3 = f32[8,128]{1,0:T(8,128)S(1)} copy-done((f32[8,128]{1,0:T(8,128)S(1)}, f32[8,128]{1,0:T(8,128)}, u32[]{:S(2)}) %copy-start.3) | copy-done | bytes 4120
  22.3 0.0 copy-start.4
  22.3 0.7 %copy-done.4 = s32[16]{0:T(128)S(1)} copy-done((s32[16]{0:T(128)S(1)}, s32[16]{0:T(128)}, u32[]{:S(2)}) %copy-start.4) | copy-done | bytes 88
  23.0 31.5 %normal_blocks.1 = (f32[13,256,256]{2,1,0:T(8,128)}, f32[1,256]{1,0:T(1,128)}) custom-call(s32[16]{0:T(128)S(1)} %copy-done.4, s32[16,8,8]{2,1,0:T(8,128)S(1)} %copy-done.2, f32[14,8,256]{2,1,0:T(8,128)S(1)} %copy-done.1, f32[5,8,1024]{2,1,0:T(8,128)S(1)} %copy-done, f32[8,128]{1,0:T(8,128)S(1)} %copy-done.3), custom_call_target="tpu_custom_call" | custom-call | tf_op jit(solution)/shard_map/normal_blocks/pallas_call | solution.py:345
Async XLA Ops:
  19.0 0.9 %copy-start = (f32[5,8,1024]{2,1,0:T(8,128)S(1)}, f32[5,8,1024]{2,1,0:T(8,128)}, u32[]{:S(2)}) copy-start(f32[5,8,1024]{2,1,0:T(8,128)} %get-tuple-element.8.tiles) | copy-start | bytes 491524
  19.9 0.9 %copy-start.1 = (f32[14,8,256]{2,1,0:T(8,128)S(1)}, f32[14,8,256]{2,1,0:T(8,128)}, u32[]{:S(2)}) copy-start(f32[14,8,256]{2,1,0:T(8,128)} %get-tuple-element.7.dips) | copy-start | bytes 344068
  20.8 0.8 %copy-start.2 = (s32[16,8,8]{2,1,0:T(8,128)S(1)}, s32[16,8,8]{2,1,0:T(8,128)}, u32[]{:S(2)}) copy-start(s32[16,8,8]{2,1,0:T(8,128)} %constant.5.clone.table) | copy-start | bytes 12292
  21.7 0.7 %copy-start.3 = (f32[8,128]{1,0:T(8,128)S(1)}, f32[8,128]{1,0:T(8,128)}, u32[]{:S(2)}) copy-start(f32[8,128]{1,0:T(8,128)} %get-tuple-element.9.origin) | copy-start | bytes 12292
  22.3 0.7 %copy-start.4 = (s32[16]{0:T(128)S(1)}, s32[16]{0:T(128)}, u32[]{:S(2)}) copy-start(s32[16]{0:T(128)} %constant.4.clone.counts) | copy-start | bytes 196
where the time goes:
time: 54.8 us; the launch traced here: 54.4 us
  Pallas kernels  47.9 us (87%)
  local copies, waits for them, and re-layouts  5.29 us (10%)
  between operations  1.3 us (2%)
    pallas_call x1, Pallas kernels, compute_call(): pl.pallas_call(kernel, out_shape=(jax.ShapeDtypeStruct((13, BS, BS), f32)...  31.5 us
    pallas_call x1, Pallas kernels, shards(): pl.pallas_call(exchange, out_shape=(jax.ShapeDtypeStruct((slots, 8, BS),...  16.4 us
    unnamed x11, local copies, waits for them, and re-layouts  5.29 us

commit v1 on v0

v1 whole, which is shorter than its diff:
```python
import functools
import math

import jax
import jax.numpy as jnp
import numpy as np
from jax import lax
from jax.experimental import pallas as pl
from jax.experimental.pallas import tpu as pltpu
from jax.sharding import PartitionSpec as P

CROSS = ((0, 0), (-1, 0), (1, 0), (0, -1), (0, 1))
OFFSETS = (
    (0, 0),
    (-1, 0),
    (1, 0),
    (0, -1),
    (0, 1),
    (-2, 0),
    (2, 0),
    (0, -2),
    (0, 2),
    (-1, -1),
    (-1, 1),
    (1, -1),
    (1, 1),
)
OBS_RADIUS = 1.06
SOURCE_RADIUS = 0.99
KERNEL_SCALE = 0.0001
HUBER_EDGE = 0.8
DEGREE = math.pi / 180.0
LAT = 16
LON = 16
BS = 256
OBS = 1024
HALF = 512
SPARE = 13
EDGE = (1.5 * (OBS_RADIUS**2 + SOURCE_RADIUS**2) - 3.0 * SOURCE_RADIUS**2) / 1.5
FOLD = 1.5 * KERNEL_SCALE * EDGE**-1.5
FEATURES = 32


def pass_rows(lat):
    rows = []
    for slot, (lat_step, lon_step) in enumerate(CROSS):
        tile = lat - lat_step
        if not 0 <= tile < LAT:
            continue
        there = [b for b in CROSS if 0 <= tile + b[0] < LAT]
        there.sort(key=lambda b: b != (lat_step, lon_step))
        blocks = [OFFSETS.index((b[0] - lat_step, b[1] - lon_step)) for b in there]
        blocks += [SPARE] * (5 - len(blocks))
        for half in range(2 if tile in (0, LAT - 1) else 1):
            rows.append((slot, half, blocks, len(there)))
    return rows


def pass_codes(lat):
    rows = pass_rows(lat)
    codes, ready = [], set(rows[0][2])
    for number, (slot, half, blocks, present) in enumerate(rows):
        after = rows[number + 1][2] if number + 1 < len(rows) else []
        fresh = [block for block in after if block not in ready]
        ready |= set(fresh)
        fresh += [SPARE] * (3 - len(fresh))
        first = sum(block << 4 * at for at, block in enumerate(blocks)) + (slot << 20) + (half << 24) + (present << 25)
        codes.append((first, sum(block << 4 * at for at, block in enumerate(fresh))))
    return codes


def by_row(lat, values):
    middle = values[LAT // 2]
    result = jnp.int32(middle)
    for row, value in enumerate(values):
        if value != middle:
            result = jnp.where(lat == row, value, result)
    return result


def positions(angles, radius):
    cosine, sine = jnp.cos(angles), jnp.sin(angles)
    ring = radius * cosine[0:1]
    return ring * cosine[1:2], ring * sine[1:2], radius * sine[0:1]


def thirds(value):
    high = value.astype(jnp.bfloat16).astype(jnp.float32)
    rest = value - high
    middle = rest.astype(jnp.bfloat16).astype(jnp.float32)
    return high, middle, rest - middle


def fill(slabs, parts, squares, flipped):
    high, middle, low = parts
    order = (high, middle, high, low, middle, high) if flipped else (high, high, middle, high, middle, low)
    for row, part in enumerate(order):
        slabs[3 * row : 3 * row + 3, :] = part
    ones = jnp.ones_like(squares[0])
    tail = (ones, ones, ones) + squares if flipped else squares + (ones, ones, ones)
    for row, part in enumerate(tail):
        slabs[18 + row : 19 + row, :] = part


def couple(squared, points, sources):
    inverse = lax.rsqrt(squared)
    second = inverse * inverse
    third = inverse * second
    fifth = third * second
    along = fifth - third
    across = fifth - third * (1.0 / 3.0)
    return [along * p - across * s for p, s in zip(points, sources)]


def prepare_source(raw, centre, slab, features, wide):
    local = raw[0:3, :] - centre
    scaled = local * (-2.0 / EDGE)
    square = jnp.sum(local * local, axis=0, keepdims=True) * (1.0 / EDGE)
    fill(slab, thirds(scaled), thirds(square), True)
    slab[24:28, :] = raw[0:4, :]
    slab[28:32, :] = jnp.zeros((4, BS), jnp.float32)
    columns = slab[...].T
    features[...] = columns.astype(jnp.bfloat16)
    for row in range(wide.shape[0]):
        column = columns[:, 24 + row : 25 + row] * (FOLD if row < 3 else 1.0)
        wide[row] = jnp.broadcast_to(column, (BS, 128))


def point_features(raw, centre, slab):
    local = raw[0:3, :] - centre
    square = jnp.sum(local * local, axis=0, keepdims=True) * (1.0 / EDGE)
    fill(slab, thirds(local), thirds(square), False)
    slab[24:32, :] = jnp.zeros((8, OBS), jnp.float32)
    return slab[...].astype(jnp.bfloat16)


def lanes_of(c, lane):
    return slice(c * HALF + lane * 128, c * HALF + lane * 128 + 128)


def exchange(count_ref, obs_ref, field_ref, dip_ref, moment_ref, dips, tiles, obs_rows, obs_features, features, wide, squared, predicted, slab_s, slab_o, send_dip, recv_dip, send_obs, recv_obs):
    lat, lon = lax.axis_index("lat"), lax.axis_index("lon")

    def inside(step):
        return (lat + step >= 0) & (lat + step < LAT)

    def device(offset):
        return (lat + offset[0], lax.rem(lon + offset[1] + LON, LON))

    barrier = pltpu.get_barrier_semaphore()
    for offset in OFFSETS[1:]:

        @pl.when(inside(offset[0]))
        def _():
            pl.semaphore_signal(barrier, inc=1, device_id=device(offset), device_id_type=pl.DeviceIdType.MESH)

    def angles(fraction):
        row = lax.broadcasted_iota(jnp.int32, fraction.shape, 0)
        index = jnp.where(row == 0, lat.astype(jnp.float32), lon.astype(jnp.float32))
        span = jnp.where(row == 0, 160.0 * DEGREE / LAT, 2.0 * math.pi / LON)
        base = jnp.where(row == 0, -80.0 * DEGREE, 0.0)
        return base + (index + fraction) * span

    for row, value in enumerate(positions(angles(dip_ref[...]), SOURCE_RADIUS)):
        dips[0, row : row + 1, :] = value
    dips[0, 3:4, :] = moment_ref[...]
    middle = positions(angles(jnp.full((2, BS), 0.5, jnp.float32)), 0.5 * (OBS_RADIUS + SOURCE_RADIUS))
    for row, value in enumerate(middle):
        dips[0, 4 + row : 5 + row, :] = value
    dips[0, 7:8, :] = jnp.zeros((1, BS), jnp.float32)

    pl.semaphore_wait(barrier, sum(inside(offset[0]).astype(jnp.int32) for offset in OFFSETS[1:]))

    def dip_copy(slot):
        step = OFFSETS[slot]
        return pltpu.make_async_remote_copy(
            src_ref=dips.at[0],
            dst_ref=dips.at[slot],
            send_sem=send_dip.at[slot],
            recv_sem=recv_dip.at[slot],
            device_id=device((-step[0], -step[1])),
            device_id_type=pl.DeviceIdType.MESH,
        )

    def obs_copy(slot):
        return pltpu.make_async_remote_copy(
            src_ref=tiles.at[0],
            dst_ref=tiles.at[slot],
            send_sem=send_obs.at[slot],
            recv_sem=recv_obs.at[slot],
            device_id=device(CROSS[slot]),
            device_id_type=pl.DeviceIdType.MESH,
        )

    for slot in range(1, len(OFFSETS)):

        @pl.when(inside(-OFFSETS[slot][0]))
        def _():
            dip_copy(slot).start()

    def dip_arrival(slot):
        @pl.when(inside(OFFSETS[slot][0]))
        def _():
            dip_copy(slot).wait_recv()

        @pl.when(jnp.logical_not(inside(OFFSETS[slot][0])))
        def _():
            dips[slot] = jnp.zeros((8, BS), jnp.float32)

    dips[SPARE] = jnp.zeros((8, BS), jnp.float32)
    for row, value in enumerate(positions(angles(obs_ref[...]), OBS_RADIUS)):
        tiles[0, row : row + 1, :] = value
    slot_index = lax.broadcasted_iota(jnp.int32, (1, OBS), 1)
    tiles[0, 6:7, :] = jnp.where(slot_index < count_ref[0, 0], 1.0, 0.0)
    tiles[0, 7:8, :] = jnp.zeros((1, OBS), jnp.float32)
    centre = dips[0, 4:7, 0:1]
    own_features = point_features(tiles[0], centre, slab_o)
    for half in range(2):
        columns = slice(half * HALF, (half + 1) * HALF)
        obs_features[half] = own_features[:, columns]
        obs_rows[half, 0:3, :] = tiles[0, 0:3, columns] * FOLD
    predicted[...] = jnp.zeros_like(predicted)
    polar = (lat == 0) | (lat == LAT - 1)
    halves = jnp.where(polar, 2, 1)

    def predict(slot):
        prepare_source(dips[slot], centre, slab_s, features, wide)

        def one_half(half, carry):
            squared[...] = jnp.dot(features[...], obs_features[half], preferred_element_type=jnp.float32)
            for lane in range(4):
                lanes = slice(lane * 128, lane * 128 + 128)
                points = [obs_rows[half, c : c + 1, lanes] for c in range(3)]
                sums = [jnp.zeros((16, 128), jnp.float32) for c in range(3)]
                for piece in range(16):
                    rows = slice(piece * 16, piece * 16 + 16)
                    values = couple(squared[rows, lanes], points, [wide[c, rows] for c in range(3)])
                    moment = wide[3, rows]
                    for c in range(3):
                        sums[c] = sums[c] + values[c] * moment
                for c in range(3):
                    predicted[half, :, lanes_of(c, lane)] += sums[c]
            return carry

        lax.fori_loop(0, halves, one_half, 0)

    def predict_slot(slot, carry):
        predict(slot)
        return carry

    lax.fori_loop(0, 1, predict_slot, 0)
    for slot in range(1, 5):
        dip_arrival(slot)
    lax.fori_loop(1, 5, predict_slot, 0)

    for half in range(2):
        for c in range(3):
            total = jnp.sum(predicted[half, :, c * HALF : (c + 1) * HALF], axis=0, keepdims=True)
            columns = slice(half * HALF, (half + 1) * HALF)
            tiles[0, 3 + c : 4 + c, columns] = field_ref[c, :, columns] - total

    for slot in range(1, len(CROSS)):

        @pl.when(inside(CROSS[slot][0]))
        def _():
            obs_copy(slot).start()

    for slot in range(5, len(OFFSETS)):
        dip_arrival(slot)

    for slot in range(1, len(OFFSETS)):

        @pl.when(inside(-OFFSETS[slot][0]))
        def _():
            dip_copy(slot).wait_send()

    for slot in range(1, len(CROSS)):

        @pl.when(inside(-CROSS[slot][0]))
        def _():
            obs_copy(slot).wait_recv()

        @pl.when(jnp.logical_not(inside(-CROSS[slot][0])))
        def _():
            tiles[slot] = jnp.zeros((8, OBS), jnp.float32)

        @pl.when(inside(CROSS[slot][0]))
        def _():
            obs_copy(slot).wait_send()


def compute(dips, tiles, gram, rhs, codes, obs_rows, obs_features, source_features, wide, squared, low, weighted, right, total, slab_s, slab_o, out_sem):
    lat = lax.axis_index("lat")
    every = [pass_codes(row) for row in range(LAT)]
    passes = by_row(lat, [len(row) for row in every])
    for number in range(max(len(row) for row in every)):
        for field in range(2):
            codes[2 * number + field] = by_row(lat, [row[number][field] if number < len(row) else 0 for row in every])
    centre = dips[0, 4:7, 0:1]

    def source_setup(slot, slab):
        prepare_source(dips[slot], centre, slab, source_features.at[slot], wide.at[slot])

    def obs_setup(slot, carry):
        raw = tiles[slot]
        features = point_features(raw, centre, slab_o)
        scaled = raw[0:3, :] * FOLD
        weight = raw[6:7, :] * HUBER_EDGE / jnp.maximum(jnp.abs(raw[3:6, :]), HUBER_EDGE)
        for half in range(2):
            columns = slice(half * HALF, (half + 1) * HALF)
            obs_features[slot, half] = features[:, columns]
            obs_rows[slot, half, 0:3, :] = scaled[:, columns]
            obs_rows[slot, half, 3:6, :] = weight[:, columns]
            obs_rows[slot, half, 6:9, :] = raw[3:6, columns]
        return carry

    lax.fori_loop(0, 5, obs_setup, 0)
    for at in range(5):
        source_setup((codes[0] >> 4 * at) & 15, slab_s.at[at])

    total[...] = jnp.zeros_like(total)
    right[...] = jnp.zeros_like(right)

    def square_block(tile, half, source, to):
        squared[to] = jnp.dot(source_features[source], obs_features[tile, half], preferred_element_type=jnp.float32)

    def couple_block(tile, half, source, position):
        for lane in range(4):
            lanes = slice(lane * 128, lane * 128 + 128)
            points = [obs_rows[tile, half, c : c + 1, lanes] for c in range(3)]
            if position == 0:
                weight = [obs_rows[tile, half, 3 + c : 4 + c, lanes] for c in range(3)]
                residual = [obs_rows[tile, half, 6 + c : 7 + c, lanes] for c in range(3)]
            for piece in range(16):
                rows = slice(piece * 16, piece * 16 + 16)
                values = couple(squared[position % 3, rows, lanes], points, [wide[source, c, rows] for c in range(3)])
                for c in range(3):
                    low[position, rows, lanes_of(c, lane)] = values[c].astype(jnp.bfloat16)
                if position == 0:
                    sums = right[rows]
                    for c in range(3):
                        value = values[c] * weight[c]
                        weighted[rows, lanes_of(c, lane)] = value.astype(jnp.bfloat16)
                        sums = sums + value * residual[c]
                    right[rows] = sums

    def add_gram(target, position):
        product = lax.dot_general(
            weighted[...], low[position], (((1,), (1,)), ((), ())), preferred_element_type=jnp.float32
        )
        total[target] = total[target] + product

    def one_pass(number, carry):
        code = codes[2 * number]
        sources = [(code >> 4 * at) & 15 for at in range(5)]
        tile, half, blocks = (code >> 20) & 15, (code >> 24) & 1, code >> 25
        fresh = codes[2 * number + 1]
        square_block(tile, half, sources[0], 0)
        for position in range(4):
            square_block(tile, half, sources[position + 1], (position + 1) % 3)
            couple_block(tile, half, sources[position], position)
            add_gram(sources[position], position)
            if position < 3:
                source_setup((fresh >> 4 * position) & 15, slab_s.at[position])

        @pl.when(blocks == 5)
        def _():
            couple_block(tile, half, sources[4], 4)
            add_gram(sources[4], 4)

        return carry

    lax.fori_loop(0, passes, one_pass, 0)
    rhs[...] = jnp.sum(right[...].T, axis=0, keepdims=True)
    copy = pltpu.make_async_copy(total.at[pl.ds(0, 13)], gram, out_sem)
    copy.start()
    copy.wait()


def shards(obs_frac, obs_field, dipole_frac, dipole_moment, obs_count):
    vmem = pl.BlockSpec(memory_space=pltpu.VMEM)
    smem = pl.BlockSpec(memory_space=pltpu.SMEM)
    slots = len(OFFSETS) + 1
    f32, low = jnp.float32, jnp.bfloat16
    dips, tiles = pl.pallas_call(
        exchange,
        out_shape=(jax.ShapeDtypeStruct((slots, 8, BS), f32), jax.ShapeDtypeStruct((5, 8, OBS), f32)),
        in_specs=[smem, vmem, vmem, vmem, vmem],
        out_specs=(vmem, vmem),
        scratch_shapes=[
            pltpu.VMEM((2, 8, HALF), f32),
            pltpu.VMEM((2, FEATURES, HALF), low),
            pltpu.VMEM((BS, FEATURES), low),
            pltpu.VMEM((4, BS, 128), f32),
            pltpu.VMEM((BS, HALF), f32),
            pltpu.VMEM((2, 16, 3 * HALF), f32),
            pltpu.VMEM((FEATURES, BS), f32),
            pltpu.VMEM((FEATURES, OBS), f32),
            pltpu.SemaphoreType.DMA((len(OFFSETS),)),
            pltpu.SemaphoreType.DMA((len(OFFSETS),)),
            pltpu.SemaphoreType.DMA((len(CROSS),)),
            pltpu.SemaphoreType.DMA((len(CROSS),)),
        ],
        compiler_params=pltpu.CompilerParams(
            collective_id=0, has_side_effects=True, vmem_limit_bytes=60 * 2**20
        ),
        name="exchange",
    )(obs_count, obs_frac[0, 0], jnp.transpose(obs_field[0], (1, 0, 2)), dipole_frac[0, 0], dipole_moment[0])
    gram, rhs = compute_call(dips, tiles)
    return gram[None, None], rhs[None]


def compute_call(dips, tiles):
    vmem = pl.BlockSpec(memory_space=pltpu.VMEM)
    slots = len(OFFSETS) + 1
    f32, low = jnp.float32, jnp.bfloat16
    return pl.pallas_call(
        compute,
        out_shape=(jax.ShapeDtypeStruct((13, BS, BS), f32), jax.ShapeDtypeStruct((1, BS), f32)),
        in_specs=[vmem, vmem],
        out_specs=(pl.BlockSpec(memory_space=pl.ANY), vmem),
        scratch_shapes=[
            pltpu.SMEM((16,), jnp.int32),
            pltpu.VMEM((5, 2, 16, HALF), f32),
            pltpu.VMEM((5, 2, FEATURES, HALF), low),
            pltpu.VMEM((slots, BS, FEATURES), low),
            pltpu.VMEM((slots, 3, BS, 128), f32),
            pltpu.VMEM((3, BS, HALF), f32),
            pltpu.VMEM((5, BS, 3 * HALF), low),
            pltpu.VMEM((BS, 3 * HALF), low),
            pltpu.VMEM((BS, 128), f32),
            pltpu.VMEM((slots, BS, BS), f32),
            pltpu.VMEM((5, FEATURES, BS), f32),
            pltpu.VMEM((FEATURES, OBS), f32),
            pltpu.SemaphoreType.DMA,
        ],
        compiler_params=pltpu.CompilerParams(vmem_limit_bytes=60 * 2**20),
        name="normal_blocks",
    )(dips, tiles)


def solution(mesh):
    in_specs = (
        P("lat", "lon", None, None),
        P("lat", "lon", None, None),
        P("lat", "lon", None, None),
        P("lat", "lon", None),
        P("lat", "lon"),
    )
    out_specs = (P("lat", "lon", None, None, None), P("lat", "lon", None))
    return jax.shard_map(shards, mesh=mesh, in_specs=in_specs, out_specs=out_specs, check_vma=False)
```

time: 54.8 us -> 51 us (0.931)
  the two profiles are of different devices: /device:TPU:1 before, /device:TPU:0 now
where the time goes in v1:
time: 51 us; the launch traced here: 50.9 us
  Pallas kernels  49.6 us (97%)
  between operations  1.29 us (3%)
    pallas_call x1, Pallas kernels, compute_call(): pl.pallas_call(compute, out_shape=(jax.ShapeDtypeStruct((13, BS, BS), f32...  25.9 us
    pallas_call x1, Pallas kernels, shards(): pl.pallas_call(exchange, out_shape=(jax.ShapeDtypeStruct((slots, 8, BS),...  23.7 us

profile of v1, /device:TPU:0, one launch (start us, length us, event | category | flops | bytes accessed | tf_op | source)
XLA Modules:
  0.0 50.9 jit_solution(13778455072803414676)
XLA Ops:
  1.3 23.7 %exchange.1 = (f32[14,8,256]{2,1,0:T(8,128)}, f32[5,8,1024]{2,1,0:T(8,128)}) custom-call(s32[1,1]{1,0:T(1,128)S(6)} %copy.7.count_ref, f32[2,1024]{1,0:T(2,128)} %bitcast.7, f32[3,1,1024]{2,1,0:T(1,128)} %bitcast.6, f32[2,256]{1,0:T(2,128)} %bitcast.8, f32[1,256]{1,0:T(1,128)} %bitcast.9), custom_call_target="tpu_custom_call" | custom-call | tf_op jit(solution)/shard_map/exchange/pallas_call | solution.py:385
  25.0 25.9 %normal_blocks.1 = (f32[13,256,256]{2,1,0:T(8,128)}, f32[1,256]{1,0:T(1,128)}) custom-call(f32[14,8,256]{2,1,0:T(8,128)} %get-tuple-element.6.dips, f32[5,8,1024]{2,1,0:T(8,128)} %get-tuple-element.7.tiles), custom_call_target="tpu_custom_call" | custom-call | tf_op jit(solution)/shard_map/normal_blocks/pallas_call | solution.py:417

commit v2 on v1

--- a/solution.py
+++ b/solution.py
@@ -36,6 +36,9 @@
 OBS = 1024
 HALF = 512
 SPARE = 13
+STEPS = 22
+UNROLL = 4
+LAST = (3, 7)
 EDGE = (1.5 * (OBS_RADIUS**2 + SOURCE_RADIUS**2) - 3.0 * SOURCE_RADIUS**2) / 1.5
 FOLD = 1.5 * KERNEL_SCALE * EDGE**-1.5
 FEATURES = 32
@@ -47,26 +50,23 @@
         tile = lat - lat_step
         if not 0 <= tile < LAT:
             continue
-        there = [b for b in CROSS if 0 <= tile + b[0] < LAT]
-        there.sort(key=lambda b: b != (lat_step, lon_step))
+        there = [b for b in CROSS if 0 <= tile + b[0] < LAT and b != (lat_step, lon_step)]
+        there.sort(key=lambda b: b[0] == 0)
         blocks = [OFFSETS.index((b[0] - lat_step, b[1] - lon_step)) for b in there]
-        blocks += [SPARE] * (5 - len(blocks))
         for half in range(2 if tile in (0, LAT - 1) else 1):
-            rows.append((slot, half, blocks, len(there)))
+            rows.append((slot, half, blocks))
     return rows
 
 
-def pass_codes(lat):
+def step_codes(lat):
     rows = pass_rows(lat)
-    codes, ready = [], set(rows[0][2])
-    for number, (slot, half, blocks, present) in enumerate(rows):
-        after = rows[number + 1][2] if number + 1 < len(rows) else []
-        fresh = [block for block in after if block not in ready]
-        ready |= set(fresh)
-        fresh += [SPARE] * (3 - len(fresh))
-        first = sum(block << 4 * at for at, block in enumerate(blocks)) + (slot << 20) + (half << 24) + (present << 25)
-        codes.append((first, sum(block << 4 * at for at, block in enumerate(fresh))))
-    return codes
+    first = [slot + (half << 4) for slot, half, blocks in rows]
+    rest = [
+        slot + (half << 4) + (number << 8) + (block << 12) + (block << 16)
+        for number, (slot, half, blocks) in enumerate(rows)
+        for block in blocks
+    ]
+    return first, [SPARE << 16] * (STEPS - len(rest)) + rest
 
 
 def by_row(lat, values):
@@ -135,6 +135,11 @@
 
 
 def lanes_of(c, lane):
+    start = (lane // 2) * 768 + c * 256 + (lane % 2) * 128
+    return slice(start, start + 128)
+
+
+def rows_of_field(c, lane):
     return slice(c * HALF + lane * 128, c * HALF + lane * 128 + 128)
 
 
@@ -223,35 +228,51 @@
     polar = (lat == 0) | (lat == LAT - 1)
     halves = jnp.where(polar, 2, 1)
 
-    def predict(slot):
-        prepare_source(dips[slot], centre, slab_s, features, wide)
-
-        def one_half(half, carry):
-            squared[...] = jnp.dot(features[...], obs_features[half], preferred_element_type=jnp.float32)
-            for lane in range(4):
-                lanes = slice(lane * 128, lane * 128 + 128)
-                points = [obs_rows[half, c : c + 1, lanes] for c in range(3)]
-                sums = [jnp.zeros((16, 128), jnp.float32) for c in range(3)]
-                for piece in range(16):
-                    rows = slice(piece * 16, piece * 16 + 16)
-                    values = couple(squared[rows, lanes], points, [wide[c, rows] for c in range(3)])
-                    moment = wide[3, rows]
-                    for c in range(3):
-                        sums[c] = sums[c] + values[c] * moment
+    def prepare(slot, to):
+        prepare_source(dips[slot], centre, slab_s, features.at[to], wide.at[to])
+
+    def predict(at, half):
+        squared[...] = jnp.dot(features[at], obs_features[half], preferred_element_type=jnp.float32)
+        for lane in range(4):
+            lanes = slice(lane * 128, lane * 128 + 128)
+            points = [obs_rows[half, c : c + 1, lanes] for c in range(3)]
+            sums = [jnp.zeros((16, 128), jnp.float32) for c in range(3)]
+            for piece in range(16):
+                rows = slice(piece * 16, piece * 16 + 16)
+                values = couple(squared[rows, lanes], points, [wide[at, c, rows] for c in range(3)])
+                moment = wide[at, 3, rows]
                 for c in range(3):
-                    predicted[half, :, lanes_of(c, lane)] += sums[c]
-            return carry
-
-        lax.fori_loop(0, halves, one_half, 0)
-
-    def predict_slot(slot, carry):
-        predict(slot)
+                    sums[c] = sums[c] + values[c] * moment
+            for c in range(3):
+                predicted[half, :, rows_of_field(c, lane)] += sums[c]
+
+    def predict_own(half, carry):
+        predict(0, half)
         return carry
 
-    lax.fori_loop(0, 1, predict_slot, 0)
+    prepare(0, 0)
+    lax.fori_loop(0, halves, predict_own, 0)
     for slot in range(1, 5):
         dip_arrival(slot)
-    lax.fori_loop(1, 5, predict_slot, 0)
+
+    third = jnp.where(lat == 0, 2, 1)
+
+    def neighbour(turn):
+        return jnp.where(turn == 0, 3, jnp.where(turn == 1, 4, jnp.where(turn == 2, third, 2)))
+
+    prepare(3, 0)
+
+    def predict_neighbour(turn, carry):
+        now = lax.rem(turn, 2)
+
+        def one_half(half, carry):
+            predict(now, half)
+            prepare(neighbour(turn + 1), 1 - now)
+            return carry
+
+        return lax.fori_loop(0, halves, one_half, carry)
+
+    lax.fori_loop(0, jnp.where(polar, 3, 4), predict_neighbour, 0)
 
     for half in range(2):
         for c in range(3):
@@ -289,13 +310,13 @@
             obs_copy(slot).wait_send()
 
 
-def compute(dips, tiles, gram, rhs, codes, obs_rows, obs_features, source_features, wide, squared, low, weighted, right, total, slab_s, slab_o, out_sem):
+def compute(dips, tiles, gram, rhs, codes, obs_rows, obs_features, source_features, wide, squared, low_a, low_b, weighted, right, total, slab_s, slab_o, out_sem):
     lat = lax.axis_index("lat")
-    every = [pass_codes(row) for row in range(LAT)]
-    passes = by_row(lat, [len(row) for row in every])
-    for number in range(max(len(row) for row in every)):
-        for field in range(2):
-            codes[2 * number + field] = by_row(lat, [row[number][field] if number < len(row) else 0 for row in every])
+    every = [step_codes(row) for row in range(LAT)]
+    passes = by_row(lat, [len(first) for first, rest in every])
+    for part, base in ((0, 0), (1, 8)):
+        for number in range(max(len(row[part]) for row in every)):
+            codes[base + number] = by_row(lat, [row[part][number] if number < len(row[part]) else 0 for row in every])
     centre = dips[0, 4:7, 0:1]
 
     def source_setup(slot, slab):
@@ -315,66 +336,119 @@
         return carry
 
     lax.fori_loop(0, 5, obs_setup, 0)
-    for at in range(5):
-        source_setup((codes[0] >> 4 * at) & 15, slab_s.at[at])
+    source_setup(0, slab_s.at[0])
+    for slot in range(1, 3):
+        source_setup(slot, slab_s.at[slot])
 
     total[...] = jnp.zeros_like(total)
     right[...] = jnp.zeros_like(right)
 
-    def square_block(tile, half, source, to):
+    def square(tile, half, source, to):
         squared[to] = jnp.dot(source_features[source], obs_features[tile, half], preferred_element_type=jnp.float32)
 
-    def couple_block(tile, half, source, position):
+    def add_gram(target, number, low):
+        product = lax.dot_general(
+            weighted[number], low[...], (((1,), (1,)), ((), ())), preferred_element_type=jnp.float32
+        )
+        total[target] = total[target] + product
+
+    def own_square(number, to):
+        code = codes[number]
+        square(code & 15, (code >> 4) & 15, 0, to)
+
+    def own_couple(number, at, low):
+        code = codes[number]
+        tile, half = code & 15, (code >> 4) & 15
+        for lane in range(4):
+            lanes = slice(lane * 128, lane * 128 + 128)
+            rows_of = [obs_rows[tile, half, c : c + 1, lanes] for c in range(9)]
+            for piece in range(16):
+                rows = slice(piece * 16, piece * 16 + 16)
+                values = couple(squared[at, rows, lanes], rows_of[0:3], [wide[0, c, rows] for c in range(3)])
+                sums = right[rows]
+                for c in range(3):
+                    low[rows, lanes_of(c, lane)] = values[c].astype(jnp.bfloat16)
+                    value = values[c] * rows_of[3 + c]
+                    weighted[number, rows, lanes_of(c, lane)] = value.astype(jnp.bfloat16)
+                    sums = sums + value * rows_of[6 + c]
+                right[rows] = sums
+
+    own_square(0, 0)
+    buffers = (low_a, low_b)
+    for number in range(5):
+        if number < 4:
+            own_square(number + 1, (number + 1) % 2)
+        if number > 0:
+            add_gram(0, number - 1, buffers[(number - 1) % 2])
+        own_couple(number, number % 2, buffers[number % 2])
+        for piece in range(2):
+            source_setup(3 + 2 * number + piece, slab_s.at[piece])
+    add_gram(0, 4, buffers[0])
+
+    def more_own(number, carry):
+        own_square(number, 0)
+        own_couple(number, 0, low_a)
+        add_gram(0, number, low_a)
+        return carry
+
+    lax.fori_loop(5, passes, more_own, 0)
+
+    def decode(step):
+        code = codes[8 + step]
+        return code & 15, (code >> 4) & 15, (code >> 8) & 15, (code >> 12) & 15, code >> 16
+
+    def square_step(step, to):
+        tile, half, number, source, target = decode(step)
+        square(tile, half, source, to)
+
+    def couple_step(step, at, low):
+        tile, half, number, source, target = decode(step)
         for lane in range(4):
             lanes = slice(lane * 128, lane * 128 + 128)
             points = [obs_rows[tile, half, c : c + 1, lanes] for c in range(3)]
-            if position == 0:
-                weight = [obs_rows[tile, half, 3 + c : 4 + c, lanes] for c in range(3)]
-                residual = [obs_rows[tile, half, 6 + c : 7 + c, lanes] for c in range(3)]
             for piece in range(16):
                 rows = slice(piece * 16, piece * 16 + 16)
-                values = couple(squared[position % 3, rows, lanes], points, [wide[source, c, rows] for c in range(3)])
+                values = couple(squared[at, rows, lanes], points, [wide[source, c, rows] for c in range(3)])
                 for c in range(3):
-                    low[position, rows, lanes_of(c, lane)] = values[c].astype(jnp.bfloat16)
-                if position == 0:
-                    sums = right[rows]
-                    for c in range(3):
-                        value = values[c] * weight[c]
-                        weighted[rows, lanes_of(c, lane)] = value.astype(jnp.bfloat16)
-                        sums = sums + value * residual[c]
-                    right[rows] = sums
-
-    def add_gram(target, position):
-        product = lax.dot_general(
-            weighted[...], low[position], (((1,), (1,)), ((), ())), preferred_element_type=jnp.float32
-        )
-        total[target] = total[target] + product
-
-    def one_pass(number, carry):
-        code = codes[2 * number]
-        sources = [(code >> 4 * at) & 15 for at in range(5)]
-        tile, half, blocks = (code >> 20) & 15, (code >> 24) & 1, code >> 25
-        fresh = codes[2 * number + 1]
-        square_block(tile, half, sources[0], 0)
-        for position in range(4):
-            square_block(tile, half, sources[position + 1], (position + 1) % 3)
-            couple_block(tile, half, sources[position], position)
-            add_gram(sources[position], position)
-            if position < 3:
-                source_setup((fresh >> 4 * position) & 15, slab_s.at[position])
-
-        @pl.when(blocks == 5)
-        def _():
-            couple_block(tile, half, sources[4], 4)
-            add_gram(sources[4], 4)
-
+                    low[rows, lanes_of(c, lane)] = values[c].astype(jnp.bfloat16)
+
+    def gram_step(step, low):
+        tile, half, number, source, target = decode(step)
+        add_gram(target, number, low)
+
+    square_step(0, 0)
+    square_step(1, 1)
+    couple_step(0, 0, low_a)
+
+    def steps_from(start, count):
+        for ahead in range(count):
+            step = start + ahead
+            before, after = (low_a, low_b) if ahead % 2 == 0 else (low_b, low_a)
+            square_step(step + 2, ahead % 2)
+            gram_step(step, before)
+            couple_step(step + 1, (ahead + 1) % 2, after)
+
+    def some_steps(group, carry):
+        steps_from(UNROLL * group, UNROLL)
         return carry
 
-    lax.fori_loop(0, passes, one_pass, 0)
+    lax.fori_loop(0, (STEPS - 2) // UNROLL, some_steps, 0)
+    def out_copy(first, count, at):
+        blocks = pl.ds(first, count)
+        return pltpu.make_async_copy(total.at[blocks], gram.at[blocks], out_sem.at[at])
+
+    early = [out_copy(0, 3, 0), out_copy(4, 3, 1), out_copy(8, 5, 2)]
+    late = [out_copy(block, 1, 3 + at) for at, block in enumerate(LAST)]
+    for copy in early:
+        copy.start()
+    gram_step(STEPS - 2, low_a)
+    late[0].start()
+    couple_step(STEPS - 1, 1, low_b)
+    gram_step(STEPS - 1, low_b)
+    late[1].start()
     rhs[...] = jnp.sum(right[...].T, axis=0, keepdims=True)
-    copy = pltpu.make_async_copy(total.at[pl.ds(0, 13)], gram, out_sem)
-    copy.start()
-    copy.wait()
+    for copy in early + late:
+        copy.wait()
 
 
 def shards(obs_frac, obs_field, dipole_frac, dipole_moment, obs_count):
@@ -390,8 +464,8 @@
         scratch_shapes=[
             pltpu.VMEM((2, 8, HALF), f32),
             pltpu.VMEM((2, FEATURES, HALF), low),
-            pltpu.VMEM((BS, FEATURES), low),
-            pltpu.VMEM((4, BS, 128), f32),
+            pltpu.VMEM((2, BS, FEATURES), low),
+            pltpu.VMEM((2, 4, BS, 128), f32),
             pltpu.VMEM((BS, HALF), f32),
             pltpu.VMEM((2, 16, 3 * HALF), f32),
             pltpu.VMEM((FEATURES, BS), f32),
@@ -420,19 +494,20 @@
         in_specs=[vmem, vmem],
         out_specs=(pl.BlockSpec(memory_space=pl.ANY), vmem),
         scratch_shapes=[
-            pltpu.SMEM((16,), jnp.int32),
+            pltpu.SMEM((32,), jnp.int32),
             pltpu.VMEM((5, 2, 16, HALF), f32),
             pltpu.VMEM((5, 2, FEATURES, HALF), low),
             pltpu.VMEM((slots, BS, FEATURES), low),
             pltpu.VMEM((slots, 3, BS, 128), f32),
-            pltpu.VMEM((3, BS, HALF), f32),
-            pltpu.VMEM((5, BS, 3 * HALF), low),
+            pltpu.VMEM((2, BS, HALF), f32),
             pltpu.VMEM((BS, 3 * HALF), low),
+            pltpu.VMEM((BS, 3 * HALF), low),
+            pltpu.VMEM((7, BS, 3 * HALF), low),
             pltpu.VMEM((BS, 128), f32),
             pltpu.VMEM((slots, BS, BS), f32),
-            pltpu.VMEM((5, FEATURES, BS), f32),
+            pltpu.VMEM((3, FEATURES, BS), f32),
             pltpu.VMEM((FEATURES, OBS), f32),
-            pltpu.SemaphoreType.DMA,
+            pltpu.SemaphoreType.DMA((5,)),
         ],
         compiler_params=pltpu.CompilerParams(vmem_limit_bytes=60 * 2**20),
         name="normal_blocks",

time: 51 us -> 46 us (0.902)
  the two profiles are of different devices: /device:TPU:0 before, /device:TPU:1 now
where the time goes in v2:
time: 46 us; the launch traced here: 45.2 us
  Pallas kernels  43.9 us (95%)
  between operations  1.29 us (3%)
    pallas_call x1, Pallas kernels, shards(): pl.pallas_call(exchange, out_shape=(jax.ShapeDtypeStruct((slots, 8, BS),...  23.5 us
    pallas_call x1, Pallas kernels, compute_call(): pl.pallas_call(compute, out_shape=(jax.ShapeDtypeStruct((13, BS, BS), f32...  20.3 us

profile of v2, /device:TPU:1, one launch (start us, length us, event | category | flops | bytes accessed | tf_op | source)
XLA Modules:
  0.0 45.2 jit_solution(9472889370483253666)
XLA Ops:
  1.3 23.5 %exchange.1 = (f32[14,8,256]{2,1,0:T(8,128)}, f32[5,8,1024]{2,1,0:T(8,128)}) custom-call(s32[1,1]{1,0:T(1,128)S(6)} %copy.7.count_ref, f32[2,1024]{1,0:T(2,128)} %bitcast.7, f32[3,1,1024]{2,1,0:T(1,128)} %bitcast.6, f32[2,256]{1,0:T(2,128)} %bitcast.8, f32[1,256]{1,0:T(1,128)} %bitcast.9), custom_call_target="tpu_custom_call" | custom-call | tf_op jit(solution)/shard_map/exchange/pallas_call | solution.py:459
  24.8 20.3 %normal_blocks.1 = (f32[13,256,256]{2,1,0:T(8,128)}, f32[1,256]{1,0:T(1,128)}) custom-call(f32[14,8,256]{2,1,0:T(8,128)} %get-tuple-element.6.dips, f32[5,8,1024]{2,1,0:T(8,128)} %get-tuple-element.7.tiles), custom_call_target="tpu_custom_call" | custom-call | tf_op jit(solution)/shard_map/normal_blocks/pallas_call | solution.py:491

commit v3 on v2

--- a/solution.py
+++ b/solution.py
@@ -36,7 +36,7 @@
 OBS = 1024
 HALF = 512
 SPARE = 13
-STEPS = 22
+STEPS = 18
 UNROLL = 4
 LAST = (3, 7)
 EDGE = (1.5 * (OBS_RADIUS**2 + SOURCE_RADIUS**2) - 3.0 * SOURCE_RADIUS**2) / 1.5
@@ -46,7 +46,7 @@
 
 def pass_rows(lat):
     rows = []
-    for slot, (lat_step, lon_step) in enumerate(CROSS):
+    for slot, (lat_step, lon_step) in list(enumerate(CROSS))[1:]:
         tile = lat - lat_step
         if not 0 <= tile < LAT:
             continue
@@ -66,7 +66,7 @@
         for number, (slot, half, blocks) in enumerate(rows)
         for block in blocks
     ]
-    return first, [SPARE << 16] * (STEPS - len(rest)) + rest
+    return first, [(SPARE << 16) + 3] * (STEPS - len(rest)) + rest
 
 
 def by_row(lat, values):
@@ -130,7 +130,7 @@
     local = raw[0:3, :] - centre
     square = jnp.sum(local * local, axis=0, keepdims=True) * (1.0 / EDGE)
     fill(slab, thirds(local), thirds(square), False)
-    slab[24:32, :] = jnp.zeros((8, OBS), jnp.float32)
+    slab[24:32, :] = jnp.zeros((8, HALF), jnp.float32)
     return slab[...].astype(jnp.bfloat16)
 
 
@@ -143,7 +143,7 @@
     return slice(c * HALF + lane * 128, c * HALF + lane * 128 + 128)
 
 
-def exchange(count_ref, obs_ref, field_ref, dip_ref, moment_ref, dips, tiles, obs_rows, obs_features, features, wide, squared, predicted, slab_s, slab_o, send_dip, recv_dip, send_obs, recv_obs):
+def exchange(count_ref, obs_ref, field_ref, dip_ref, moment_ref, dips, tiles, partial, rhs, obs_rows, obs_features, features, wide, squared, predicted, low, weighted, right, total, slab_s, slab_o, send_dip, recv_dip, send_obs, recv_obs, out_sem):
     lat, lon = lax.axis_index("lat"), lax.axis_index("lon")
 
     def inside(step):
@@ -187,12 +187,15 @@
             device_id_type=pl.DeviceIdType.MESH,
         )
 
-    def obs_copy(slot):
+    def polar(row):
+        return (row == 0) | (row == LAT - 1)
+
+    def obs_copy(slot, half):
         return pltpu.make_async_remote_copy(
-            src_ref=tiles.at[0],
-            dst_ref=tiles.at[slot],
-            send_sem=send_obs.at[slot],
-            recv_sem=recv_obs.at[slot],
+            src_ref=tiles.at[0, half],
+            dst_ref=tiles.at[slot, half],
+            send_sem=send_obs.at[slot, half],
+            recv_sem=recv_obs.at[slot, half],
             device_id=device(CROSS[slot]),
             device_id_type=pl.DeviceIdType.MESH,
         )
@@ -213,25 +216,27 @@
             dips[slot] = jnp.zeros((8, BS), jnp.float32)
 
     dips[SPARE] = jnp.zeros((8, BS), jnp.float32)
-    for row, value in enumerate(positions(angles(obs_ref[...]), OBS_RADIUS)):
-        tiles[0, row : row + 1, :] = value
+    place = positions(angles(obs_ref[...]), OBS_RADIUS)
     slot_index = lax.broadcasted_iota(jnp.int32, (1, OBS), 1)
-    tiles[0, 6:7, :] = jnp.where(slot_index < count_ref[0, 0], 1.0, 0.0)
-    tiles[0, 7:8, :] = jnp.zeros((1, OBS), jnp.float32)
+    present = jnp.where(slot_index < count_ref[0, 0], 1.0, 0.0)
     centre = dips[0, 4:7, 0:1]
-    own_features = point_features(tiles[0], centre, slab_o)
     for half in range(2):
         columns = slice(half * HALF, (half + 1) * HALF)
-        obs_features[half] = own_features[:, columns]
-        obs_rows[half, 0:3, :] = tiles[0, 0:3, columns] * FOLD
+        for row, value in enumerate(place):
+            tiles[0, half, row : row + 1, :] = value[:, columns]
+        tiles[0, half, 6:7, :] = present[:, columns]
+        tiles[0, half, 7:8, :] = jnp.zeros((1, HALF), jnp.float32)
+        obs_features[half] = point_features(tiles[0, half], centre, slab_o)
+        obs_rows[half, 0:3, :] = tiles[0, half, 0:3, :] * FOLD
     predicted[...] = jnp.zeros_like(predicted)
-    polar = (lat == 0) | (lat == LAT - 1)
-    halves = jnp.where(polar, 2, 1)
+    total[...] = jnp.zeros_like(total)
+    right[...] = jnp.zeros_like(right)
+    halves = jnp.where(polar(lat), 2, 1)
 
     def prepare(slot, to):
         prepare_source(dips[slot], centre, slab_s, features.at[to], wide.at[to])
 
-    def predict(at, half):
+    def predict(at, half, slot):
         squared[...] = jnp.dot(features[at], obs_features[half], preferred_element_type=jnp.float32)
         for lane in range(4):
             lanes = slice(lane * 128, lane * 128 + 128)
@@ -243,14 +248,15 @@
                 moment = wide[at, 3, rows]
                 for c in range(3):
                     sums[c] = sums[c] + values[c] * moment
+                    low[half, slot, rows, lanes_of(c, lane)] = values[c].astype(jnp.bfloat16)
             for c in range(3):
                 predicted[half, :, rows_of_field(c, lane)] += sums[c]
 
     def predict_own(half, carry):
-        predict(0, half)
+        predict(2, half, 0)
         return carry
 
-    prepare(0, 0)
+    prepare(0, 2)
     lax.fori_loop(0, halves, predict_own, 0)
     for slot in range(1, 5):
         dip_arrival(slot)
@@ -266,25 +272,64 @@
         now = lax.rem(turn, 2)
 
         def one_half(half, carry):
-            predict(now, half)
+            predict(now, half, neighbour(turn))
             prepare(neighbour(turn + 1), 1 - now)
             return carry
 
         return lax.fori_loop(0, halves, one_half, carry)
 
-    lax.fori_loop(0, jnp.where(polar, 3, 4), predict_neighbour, 0)
+    lax.fori_loop(0, jnp.where(polar(lat), 3, 4), predict_neighbour, 0)
 
     for half in range(2):
+        columns = slice(half * HALF, (half + 1) * HALF)
         for c in range(3):
-            total = jnp.sum(predicted[half, :, c * HALF : (c + 1) * HALF], axis=0, keepdims=True)
-            columns = slice(half * HALF, (half + 1) * HALF)
-            tiles[0, 3 + c : 4 + c, columns] = field_ref[c, :, columns] - total
+            sums = jnp.sum(predicted[half, :, c * HALF : (c + 1) * HALF], axis=0, keepdims=True)
+            tiles[0, half, 3 + c : 4 + c, :] = field_ref[c, :, columns] - sums
 
     for slot in range(1, len(CROSS)):
 
         @pl.when(inside(CROSS[slot][0]))
         def _():
-            obs_copy(slot).start()
+            obs_copy(slot, 0).start()
+
+            @pl.when(polar(lat))
+            def _():
+                obs_copy(slot, 1).start()
+
+    for half in range(2):
+        obs_rows[half, 3:6, :] = tiles[0, half, 6:7, :] * HUBER_EDGE / jnp.maximum(jnp.abs(tiles[0, half, 3:6, :]), HUBER_EDGE)
+
+    def own_share(half, carry):
+        squared[...] = jnp.dot(features[2], obs_features[half], preferred_element_type=jnp.float32)
+        for lane in range(4):
+            lanes = slice(lane * 128, lane * 128 + 128)
+            points = [obs_rows[half, c : c + 1, lanes] for c in range(3)]
+            weight = [obs_rows[half, 3 + c : 4 + c, lanes] for c in range(3)]
+            residual = [tiles[0, half, 3 + c : 4 + c, lanes] for c in range(3)]
+            for piece in range(16):
+                rows = slice(piece * 16, piece * 16 + 16)
+                values = couple(squared[rows, lanes], points, [wide[2, c, rows] for c in range(3)])
+                sums = right[rows]
+                for c in range(3):
+                    value = values[c] * weight[c]
+                    weighted[rows, lanes_of(c, lane)] = value.astype(jnp.bfloat16)
+                    sums = sums + value * residual[c]
+                right[rows] = sums
+
+        def share(turn, inner):
+            slot = jnp.where(turn == 0, 0, neighbour(turn - 1))
+            product = lax.dot_general(
+                weighted[...], low[half, slot], (((1,), (1,)), ((), ())), preferred_element_type=jnp.float32
+            )
+            total[slot] = total[slot] + product
+            return inner
+
+        return lax.fori_loop(0, jnp.where(polar(lat), 4, 5), share, carry)
+
+    lax.fori_loop(0, halves, own_share, 0)
+    rhs[...] = jnp.sum(right[...].T, axis=0, keepdims=True)
+    partial_copy = pltpu.make_async_copy(total, partial, out_sem)
+    partial_copy.start()
 
     for slot in range(5, len(OFFSETS)):
         dip_arrival(slot)
@@ -296,51 +341,56 @@
             dip_copy(slot).wait_send()
 
     for slot in range(1, len(CROSS)):
-
-        @pl.when(inside(-CROSS[slot][0]))
-        def _():
-            obs_copy(slot).wait_recv()
-
-        @pl.when(jnp.logical_not(inside(-CROSS[slot][0])))
-        def _():
-            tiles[slot] = jnp.zeros((8, OBS), jnp.float32)
-
-        @pl.when(inside(CROSS[slot][0]))
-        def _():
-            obs_copy(slot).wait_send()
-
-
-def compute(dips, tiles, gram, rhs, codes, obs_rows, obs_features, source_features, wide, squared, low_a, low_b, weighted, right, total, slab_s, slab_o, out_sem):
+        step = CROSS[slot][0]
+
+        @pl.when(inside(-step))
+        def _():
+            obs_copy(slot, 0).wait_recv()
+
+            @pl.when(polar(lat - step))
+            def _():
+                obs_copy(slot, 1).wait_recv()
+
+        @pl.when(inside(step))
+        def _():
+            obs_copy(slot, 0).wait_send()
+
+            @pl.when(polar(lat))
+            def _():
+                obs_copy(slot, 1).wait_send()
+
+    partial_copy.wait()
+
+
+def compute(dips, tiles, partial, share, gram, rhs, codes, obs_rows, obs_features, source_features, wide, squared, low_a, low_b, weighted, right, total, slab_s, slab_o, out_sem, in_sem):
     lat = lax.axis_index("lat")
     every = [step_codes(row) for row in range(LAT)]
     passes = by_row(lat, [len(first) for first, rest in every])
     for part, base in ((0, 0), (1, 8)):
         for number in range(max(len(row[part]) for row in every)):
             codes[base + number] = by_row(lat, [row[part][number] if number < len(row[part]) else 0 for row in every])
+    partial_copy = pltpu.make_async_copy(partial, total.at[pl.ds(0, 5)], in_sem)
+    partial_copy.start()
     centre = dips[0, 4:7, 0:1]
 
     def source_setup(slot, slab):
         prepare_source(dips[slot], centre, slab, source_features.at[slot], wide.at[slot])
 
     def obs_setup(slot, carry):
-        raw = tiles[slot]
-        features = point_features(raw, centre, slab_o)
-        scaled = raw[0:3, :] * FOLD
-        weight = raw[6:7, :] * HUBER_EDGE / jnp.maximum(jnp.abs(raw[3:6, :]), HUBER_EDGE)
         for half in range(2):
-            columns = slice(half * HALF, (half + 1) * HALF)
-            obs_features[slot, half] = features[:, columns]
-            obs_rows[slot, half, 0:3, :] = scaled[:, columns]
-            obs_rows[slot, half, 3:6, :] = weight[:, columns]
-            obs_rows[slot, half, 6:9, :] = raw[3:6, columns]
+            raw = tiles[slot, half]
+            obs_features[slot, half] = point_features(raw, centre, slab_o)
+            obs_rows[slot, half, 0:3, :] = raw[0:3, :] * FOLD
+            obs_rows[slot, half, 3:6, :] = raw[6:7, :] * HUBER_EDGE / jnp.maximum(jnp.abs(raw[3:6, :]), HUBER_EDGE)
+            obs_rows[slot, half, 6:9, :] = raw[3:6, :]
         return carry
 
-    lax.fori_loop(0, 5, obs_setup, 0)
+    lax.fori_loop(1, 5, obs_setup, 0)
     source_setup(0, slab_s.at[0])
     for slot in range(1, 3):
         source_setup(slot, slab_s.at[slot])
 
-    total[...] = jnp.zeros_like(total)
+    total[5:] = jnp.zeros_like(total[5:])
     right[...] = jnp.zeros_like(right)
 
     def square(tile, half, source, to):
@@ -375,15 +425,19 @@
 
     own_square(0, 0)
     buffers = (low_a, low_b)
-    for number in range(5):
-        if number < 4:
+    fresh = 3
+    for number in range(4):
+        if number < 3:
             own_square(number + 1, (number + 1) % 2)
+        if number == 1:
+            partial_copy.wait()
         if number > 0:
             add_gram(0, number - 1, buffers[(number - 1) % 2])
         own_couple(number, number % 2, buffers[number % 2])
-        for piece in range(2):
-            source_setup(3 + 2 * number + piece, slab_s.at[piece])
-    add_gram(0, 4, buffers[0])
+        for piece in range(3 if number < 2 else 2):
+            source_setup(fresh, slab_s.at[piece])
+            fresh += 1
+    add_gram(0, 3, buffers[1])
 
     def more_own(number, carry):
         own_square(number, 0)
@@ -391,7 +445,7 @@
         add_gram(0, number, low_a)
         return carry
 
-    lax.fori_loop(5, passes, more_own, 0)
+    lax.fori_loop(4, passes, more_own, 0)
 
     def decode(step):
         code = codes[8 + step]
@@ -446,7 +500,7 @@
     couple_step(STEPS - 1, 1, low_b)
     gram_step(STEPS - 1, low_b)
     late[1].start()
-    rhs[...] = jnp.sum(right[...].T, axis=0, keepdims=True)
+    rhs[...] = share[...] + jnp.sum(right[...].T, axis=0, keepdims=True)
     for copy in early + late:
         copy.wait()
 
@@ -456,42 +510,52 @@
     smem = pl.BlockSpec(memory_space=pltpu.SMEM)
     slots = len(OFFSETS) + 1
     f32, low = jnp.float32, jnp.bfloat16
-    dips, tiles = pl.pallas_call(
+    dips, tiles, partial, share = pl.pallas_call(
         exchange,
-        out_shape=(jax.ShapeDtypeStruct((slots, 8, BS), f32), jax.ShapeDtypeStruct((5, 8, OBS), f32)),
+        out_shape=(
+            jax.ShapeDtypeStruct((slots, 8, BS), f32),
+            jax.ShapeDtypeStruct((5, 2, 8, HALF), f32),
+            jax.ShapeDtypeStruct((5, BS, BS), f32),
+            jax.ShapeDtypeStruct((1, BS), f32),
+        ),
         in_specs=[smem, vmem, vmem, vmem, vmem],
-        out_specs=(vmem, vmem),
+        out_specs=(vmem, vmem, pl.BlockSpec(memory_space=pl.ANY), vmem),
         scratch_shapes=[
             pltpu.VMEM((2, 8, HALF), f32),
             pltpu.VMEM((2, FEATURES, HALF), low),
-            pltpu.VMEM((2, BS, FEATURES), low),
-            pltpu.VMEM((2, 4, BS, 128), f32),
+            pltpu.VMEM((3, BS, FEATURES), low),
+            pltpu.VMEM((3, 4, BS, 128), f32),
             pltpu.VMEM((BS, HALF), f32),
             pltpu.VMEM((2, 16, 3 * HALF), f32),
+            pltpu.VMEM((2, 5, BS, 3 * HALF), low),
+            pltpu.VMEM((BS, 3 * HALF), low),
+            pltpu.VMEM((BS, 128), f32),
+            pltpu.VMEM((5, BS, BS), f32),
             pltpu.VMEM((FEATURES, BS), f32),
-            pltpu.VMEM((FEATURES, OBS), f32),
+            pltpu.VMEM((FEATURES, HALF), f32),
             pltpu.SemaphoreType.DMA((len(OFFSETS),)),
             pltpu.SemaphoreType.DMA((len(OFFSETS),)),
-            pltpu.SemaphoreType.DMA((len(CROSS),)),
-            pltpu.SemaphoreType.DMA((len(CROSS),)),
+            pltpu.SemaphoreType.DMA((len(CROSS), 2)),
+            pltpu.SemaphoreType.DMA((len(CROSS), 2)),
+            pltpu.SemaphoreType.DMA,
         ],
         compiler_params=pltpu.CompilerParams(
             collective_id=0, has_side_effects=True, vmem_limit_bytes=60 * 2**20
         ),
         name="exchange",
     )(obs_count, obs_frac[0, 0], jnp.transpose(obs_field[0], (1, 0, 2)), dipole_frac[0, 0], dipole_moment[0])
-    gram, rhs = compute_call(dips, tiles)
+    gram, rhs = compute_call(dips, tiles, partial, share)
     return gram[None, None], rhs[None]
 
 
-def compute_call(dips, tiles):
+def compute_call(dips, tiles, partial, share):
     vmem = pl.BlockSpec(memory_space=pltpu.VMEM)
     slots = len(OFFSETS) + 1
     f32, low = jnp.float32, jnp.bfloat16
     return pl.pallas_call(
         compute,
         out_shape=(jax.ShapeDtypeStruct((13, BS, BS), f32), jax.ShapeDtypeStruct((1, BS), f32)),
-        in_specs=[vmem, vmem],
+        in_specs=[vmem, vmem, pl.BlockSpec(memory_space=pl.ANY), vmem],
         out_specs=(pl.BlockSpec(memory_space=pl.ANY), vmem),
         scratch_shapes=[
             pltpu.SMEM((32,), jnp.int32),
@@ -502,16 +566,17 @@
             pltpu.VMEM((2, BS, HALF), f32),
             pltpu.VMEM((BS, 3 * HALF), low),
             pltpu.VMEM((BS, 3 * HALF), low),
-            pltpu.VMEM((7, BS, 3 * HALF), low),
+            pltpu.VMEM((5, BS, 3 * HALF), low),
             pltpu.VMEM((BS, 128), f32),
             pltpu.VMEM((slots, BS, BS), f32),
             pltpu.VMEM((3, FEATURES, BS), f32),
-            pltpu.VMEM((FEATURES, OBS), f32),
+            pltpu.VMEM((FEATURES, HALF), f32),
             pltpu.SemaphoreType.DMA((5,)),
+            pltpu.SemaphoreType.DMA,
         ],
         compiler_params=pltpu.CompilerParams(vmem_limit_bytes=60 * 2**20),
         name="normal_blocks",
-    )(dips, tiles)
+    )(dips, tiles, partial, share)
 
 
 def solution(mesh):

time: 46 us -> 42.6 us (0.926); the launches traced: 45.2 us -> 42.5 us
  Pallas kernels: 43.9 us -> 41.2 us
    pallas_call x1, Pallas kernels: 20.3 us -> 17.6 us  [compute_call(): pl.pallas_call(compute, out_shape=(jax.ShapeDtypeStruct((13, BS, BS), f32...]
where the time goes in v3:
time: 42.6 us; the launch traced here: 42.5 us
  Pallas kernels  41.2 us (97%)
  between operations  1.29 us (3%)
    pallas_call x1, Pallas kernels, shards(): pl.pallas_call(exchange, out_shape=(jax.ShapeDtypeStruct((slots, 8, BS),...  23.6 us
    pallas_call x1, Pallas kernels, compute_call(): pl.pallas_call(compute, out_shape=(jax.ShapeDtypeStruct((13, BS, BS), f32...  17.6 us

profile of v3, /device:TPU:1, one launch (start us, length us, event | category | flops | bytes accessed | tf_op | source)
XLA Modules:
  0.0 42.5 jit_solution(11988216803306409215)
XLA Ops:
  1.3 23.6 %exchange.1 = (f32[14,8,256]{2,1,0:T(8,128)}, f32[5,2,8,512]{3,2,1,0:T(8,128)}, f32[5,256,256]{2,1,0:T(8,128)}, f32[1,256]{1,0:T(1,128)}) custom-call(s32[1,1]{1,0:T(1,128)S(6)} %copy.7.count_ref, f32[2,1024]{1,0:T(2,128)} %bitcast.7, f32[3,1,1024]{2,1,0:T(1,128)} %bitcast.6, f32[2,256]{1,0:T(2,128)} %bitcast.8, f32[1,256]{1,0:T(1,128)} %bitcast.9), custom_call_target="tpu_custom_call" | custom-call | tf_op jit(solution)/shard_map/exchange/pallas_call | solution.py:513
  24.9 17.6 %normal_blocks.1 = (f32[13,256,256]{2,1,0:T(8,128)}, f32[1,256]{1,0:T(1,128)}) custom-call(f32[14,8,256]{2,1,0:T(8,128)} %get-tuple-element.8.dips, f32[5,2,8,512]{3,2,1,0:T(8,128)} %get-tuple-element.9.tiles, f32[5,256,256]{2,1,0:T(8,128)} %get-tuple-element.10.partial, f32[1,256]{1,0:T(1,128)} %get-tuple-element.11.share), custom_call_target="tpu_custom_call" | custom-call | tf_op jit(solution)/shard_map/normal_blocks/pallas_call | solution.py:555

commit v4 on v3

--- a/solution.py
+++ b/solution.py
@@ -143,8 +143,12 @@
     return slice(c * HALF + lane * 128, c * HALF + lane * 128 + 128)
 
 
-def exchange(count_ref, obs_ref, field_ref, dip_ref, moment_ref, dips, tiles, partial, rhs, obs_rows, obs_features, features, wide, squared, predicted, low, weighted, right, total, slab_s, slab_o, send_dip, recv_dip, send_obs, recv_obs, out_sem):
+def exchange(count_ref, obs_in, field_in, dip_in, moment_in, dips, tiles, partial, rhs, obs_rows, obs_features, features, wide, squared, predicted, low, weighted, right, total, slab_s, slab_o, send_dip, recv_dip, send_obs, recv_obs, out_sem, obs_ref, field_ref, dip_ref, moment_ref, in_sem):
     lat, lon = lax.axis_index("lat"), lax.axis_index("lon")
+    pairs = ((dip_in, dip_ref), (moment_in, moment_ref), (obs_in, obs_ref), (field_in, field_ref))
+    loads = [pltpu.make_async_copy(source, target, in_sem.at[at]) for at, (source, target) in enumerate(pairs)]
+    for load in loads:
+        load.start()
 
     def inside(step):
         return (lat + step >= 0) & (lat + step < LAT)
@@ -166,6 +170,8 @@
         base = jnp.where(row == 0, -80.0 * DEGREE, 0.0)
         return base + (index + fraction) * span
 
+    for load in loads[:2]:
+        load.wait()
     for row, value in enumerate(positions(angles(dip_ref[...]), SOURCE_RADIUS)):
         dips[0, row : row + 1, :] = value
     dips[0, 3:4, :] = moment_ref[...]
@@ -216,6 +222,8 @@
             dips[slot] = jnp.zeros((8, BS), jnp.float32)
 
     dips[SPARE] = jnp.zeros((8, BS), jnp.float32)
+    for load in loads[2:]:
+        load.wait()
     place = positions(angles(obs_ref[...]), OBS_RADIUS)
     slot_index = lax.broadcasted_iota(jnp.int32, (1, OBS), 1)
     present = jnp.where(slot_index < count_ref[0, 0], 1.0, 0.0)
@@ -272,8 +280,8 @@
         now = lax.rem(turn, 2)
 
         def one_half(half, carry):
+            prepare(neighbour(turn + 1), 1 - now)
             predict(now, half, neighbour(turn))
-            prepare(neighbour(turn + 1), 1 - now)
             return carry
 
         return lax.fori_loop(0, halves, one_half, carry)
@@ -433,10 +441,10 @@
             partial_copy.wait()
         if number > 0:
             add_gram(0, number - 1, buffers[(number - 1) % 2])
-        own_couple(number, number % 2, buffers[number % 2])
         for piece in range(3 if number < 2 else 2):
             source_setup(fresh, slab_s.at[piece])
             fresh += 1
+        own_couple(number, number % 2, buffers[number % 2])
     add_gram(0, 3, buffers[1])
 
     def more_own(number, carry):
@@ -507,7 +515,6 @@
 
 def shards(obs_frac, obs_field, dipole_frac, dipole_moment, obs_count):
     vmem = pl.BlockSpec(memory_space=pltpu.VMEM)
-    smem = pl.BlockSpec(memory_space=pltpu.SMEM)
     slots = len(OFFSETS) + 1
     f32, low = jnp.float32, jnp.bfloat16
     dips, tiles, partial, share = pl.pallas_call(
@@ -518,7 +525,7 @@
             jax.ShapeDtypeStruct((5, BS, BS), f32),
             jax.ShapeDtypeStruct((1, BS), f32),
         ),
-        in_specs=[smem, vmem, vmem, vmem, vmem],
+        in_specs=[pl.BlockSpec(memory_space=pltpu.SMEM)] + [pl.BlockSpec(memory_space=pl.ANY)] * 4,
         out_specs=(vmem, vmem, pl.BlockSpec(memory_space=pl.ANY), vmem),
         scratch_shapes=[
             pltpu.VMEM((2, 8, HALF), f32),
@@ -538,6 +545,11 @@
             pltpu.SemaphoreType.DMA((len(CROSS), 2)),
             pltpu.SemaphoreType.DMA((len(CROSS), 2)),
             pltpu.SemaphoreType.DMA,
+            pltpu.VMEM((2, OBS), f32),
+            pltpu.VMEM((3, 1, OBS), f32),
+            pltpu.VMEM((2, BS), f32),
+            pltpu.VMEM((1, BS), f32),
+            pltpu.SemaphoreType.DMA((4,)),
         ],
         compiler_params=pltpu.CompilerParams(
             collective_id=0, has_side_effects=True, vmem_limit_bytes=60 * 2**20

time: 42.6 us -> 41.8 us (0.981)
  Pallas kernels: 41.2 us -> 40.4 us
    pallas_call x1, Pallas kernels: 23.6 us -> 22.8 us  [shards(): pl.pallas_call(exchange, out_shape=(jax.ShapeDtypeStruct((slots, 8, BS),...]
where the time goes in v4:
time: 41.8 us; the launch traced here: 41.6 us
  Pallas kernels  40.4 us (97%)
  between operations  1.29 us (3%)
    pallas_call x1, Pallas kernels, shards(): pl.pallas_call(exchange, out_shape=(jax.ShapeDtypeStruct((slots, 8, BS),...  22.8 us
    pallas_call x1, Pallas kernels, compute_call(): pl.pallas_call(compute, out_shape=(jax.ShapeDtypeStruct((13, BS, BS), f32...  17.6 us

profile of v4, /device:TPU:1, one launch (start us, length us, event | category | flops | bytes accessed | tf_op | source)
XLA Modules:
  0.0 41.6 jit_solution(9870681228424336291)
XLA Ops:
  1.3 22.8 %exchange.1 = (f32[14,8,256]{2,1,0:T(8,128)}, f32[5,2,8,512]{3,2,1,0:T(8,128)}, f32[5,256,256]{2,1,0:T(8,128)}, f32[1,256]{1,0:T(1,128)}) custom-call(s32[1,1]{1,0:T(1,128)S(6)} %copy.7.count_ref, f32[2,1024]{1,0:T(2,128)} %bitcast.7, f32[3,1,1024]{2,1,0:T(1,128)} %bitcast.6, f32[2,256]{1,0:T(2,128)} %bitcast.8, f32[1,256]{1,0:T(1,128)} %bitcast.9), custom_call_target="tpu_custom_call" | custom-call | tf_op jit(solution)/shard_map/exchange/pallas_call | solution.py:520
  24.0 17.6 %normal_blocks.1 = (f32[13,256,256]{2,1,0:T(8,128)}, f32[1,256]{1,0:T(1,128)}) custom-call(f32[14,8,256]{2,1,0:T(8,128)} %get-tuple-element.8.dips, f32[5,2,8,512]{3,2,1,0:T(8,128)} %get-tuple-element.9.tiles, f32[5,256,256]{2,1,0:T(8,128)} %get-tuple-element.10.partial, f32[1,256]{1,0:T(1,128)} %get-tuple-element.11.share), custom_call_target="tpu_custom_call" | custom-call | tf_op jit(solution)/shard_map/normal_blocks/pallas_call | solution.py:567

commit v5 on v4

--- a/solution.py
+++ b/solution.py
@@ -294,7 +294,7 @@
             sums = jnp.sum(predicted[half, :, c * HALF : (c + 1) * HALF], axis=0, keepdims=True)
             tiles[0, half, 3 + c : 4 + c, :] = field_ref[c, :, columns] - sums
 
-    for slot in range(1, len(CROSS)):
+    for slot in (3, 4, 1, 2):
 
         @pl.when(inside(CROSS[slot][0]))
         def _():
@@ -306,6 +306,13 @@
 
     for half in range(2):
         obs_rows[half, 3:6, :] = tiles[0, half, 6:7, :] * HUBER_EDGE / jnp.maximum(jnp.abs(tiles[0, half, 3:6, :]), HUBER_EDGE)
+
+    def partial_copy(slot):
+        return pltpu.make_async_copy(total.at[slot], partial.at[slot], out_sem.at[slot])
+
+    @pl.when(polar(lat))
+    def _():
+        partial_copy(jnp.where(lat == 0, 1, 2)).start()
 
     def own_share(half, carry):
         squared[...] = jnp.dot(features[2], obs_features[half], preferred_element_type=jnp.float32)
@@ -330,15 +337,17 @@
                 weighted[...], low[half, slot], (((1,), (1,)), ((), ())), preferred_element_type=jnp.float32
             )
             total[slot] = total[slot] + product
+
+            @pl.when(half == halves - 1)
+            def _():
+                partial_copy(slot).start()
+
             return inner
 
         return lax.fori_loop(0, jnp.where(polar(lat), 4, 5), share, carry)
 
     lax.fori_loop(0, halves, own_share, 0)
     rhs[...] = jnp.sum(right[...].T, axis=0, keepdims=True)
-    partial_copy = pltpu.make_async_copy(total, partial, out_sem)
-    partial_copy.start()
-
     for slot in range(5, len(OFFSETS)):
         dip_arrival(slot)
 
@@ -367,7 +376,8 @@
             def _():
                 obs_copy(slot, 1).wait_send()
 
-    partial_copy.wait()
+    for slot in range(5):
+        partial_copy(slot).wait()
 
 
 def compute(dips, tiles, partial, share, gram, rhs, codes, obs_rows, obs_features, source_features, wide, squared, low_a, low_b, weighted, right, total, slab_s, slab_o, out_sem, in_sem):
@@ -544,7 +554,7 @@
             pltpu.SemaphoreType.DMA((len(OFFSETS),)),
             pltpu.SemaphoreType.DMA((len(CROSS), 2)),
             pltpu.SemaphoreType.DMA((len(CROSS), 2)),
-            pltpu.SemaphoreType.DMA,
+            pltpu.SemaphoreType.DMA((5,)),
             pltpu.VMEM((2, OBS), f32),
             pltpu.VMEM((3, 1, OBS), f32),
             pltpu.VMEM((2, BS), f32),

time: 41.8 us -> 41.8 us (level)
  no operation moved by 1% of the time
where the time goes in v5:
time: 41.8 us; the launch traced here: 41.7 us
  Pallas kernels  40.4 us (97%)
  between operations  1.29 us (3%)
    pallas_call x1, Pallas kernels, shards(): pl.pallas_call(exchange, out_shape=(jax.ShapeDtypeStruct((slots, 8, BS),...  22.8 us
    pallas_call x1, Pallas kernels, compute_call(): pl.pallas_call(compute, out_shape=(jax.ShapeDtypeStruct((13, BS, BS), f32...  17.6 us

profile of v5, /device:TPU:1, one launch (start us, length us, event | category | flops | bytes accessed | tf_op | source)
XLA Modules:
  0.0 41.7 jit_solution(13785674691398470069)
XLA Ops:
  1.3 22.8 %exchange.1 = (f32[14,8,256]{2,1,0:T(8,128)}, f32[5,2,8,512]{3,2,1,0:T(8,128)}, f32[5,256,256]{2,1,0:T(8,128)}, f32[1,256]{1,0:T(1,128)}) custom-call(s32[1,1]{1,0:T(1,128)S(6)} %copy.7.count_ref, f32[2,1024]{1,0:T(2,128)} %bitcast.7, f32[3,1,1024]{2,1,0:T(1,128)} %bitcast.6, f32[2,256]{1,0:T(2,128)} %bitcast.8, f32[1,256]{1,0:T(1,128)} %bitcast.9), custom_call_target="tpu_custom_call" | custom-call | tf_op jit(solution)/shard_map/exchange/pallas_call | solution.py:530
  24.1 17.6 %normal_blocks.1 = (f32[13,256,256]{2,1,0:T(8,128)}, f32[1,256]{1,0:T(1,128)}) custom-call(f32[14,8,256]{2,1,0:T(8,128)} %get-tuple-element.8.dips, f32[5,2,8,512]{3,2,1,0:T(8,128)} %get-tuple-element.9.tiles, f32[5,256,256]{2,1,0:T(8,128)} %get-tuple-element.10.partial, f32[1,256]{1,0:T(1,128)} %get-tuple-element.11.share), custom_call_target="tpu_custom_call" | custom-call | tf_op jit(solution)/shard_map/normal_blocks/pallas_call | solution.py:577
